TPU v7x, 128 devices: a whole 4x4x4 slice. The times are simulated.
128 devices in a mesh: section: 16 (over y_hi, x, core), dp: 8 (over z, y_lo).
Axes of the slice: x: 4, y: 4 (y_hi: 2, y_lo: 2; y = y_hi * 2 + y_lo), z: 4, core: 2. Of those that a mesh axis runs over, the one named last changes fastest.
Arguments:
- cotangent: bfloat16 [2, 128, 4096], P(None, None, 'dp'), may hold values from -3 to 3
- inputs: bfloat16 [16, 2, 128, 4096], P('section', None, None, 'dp'), may hold values from -6 to 6
- inv_rms: float32 [16, 2, 128], P('section'), may hold values from 0.1 to 0.4
- gain: float32 [16, 4096], P('section'), may hold values from 0.1 to 1.9
- weight: bfloat16 [16, 4096, 4096], P('section', None, 'dp'), may hold values from -0.09375 to 0.09375
Outputs:
- grad_in: bfloat16 [16, 2, 128, 4096], P('section', None, None, 'dp')
- weight_grad: float32 [16, 4096, 4096], P('section', None, 'dp')
- gain_grad: float32 [16, 4096], P('section', 'dp')
- row_dot: float32 [16, 2, 128], P('section')
All inputs are finite; a program needn't handle non-finite values.
Results may differ from a plain program's by a relative error of at most 0.035.
Values may be sent and summed in bfloat16 or wider, within the bound.
A program may use at most 64 MiB of HBM per device.

v0:
```python
import jax
import jax.numpy as jnp
from jax import lax
from jax.sharding import PartitionSpec as P


def shifted(block, axis, distance):
    devices = range(lax.axis_size(axis))
    route = [(i - distance, i) for i in devices if i - distance in devices]
    return lax.ppermute(block, axis, route)


def body(cotangent, inputs, inv_rms, gain, weight):
    micro, rows, cols = cotangent.shape
    sections = lax.axis_size("section")
    section = lax.axis_index("section")
    hidden_width = cols * lax.axis_size("dp")
    root_width = float(hidden_width) ** 0.5
    token_scale = float(micro * rows) ** (-0.5)
    first_col = lax.axis_index("dp") * cols
    w_local = weight[0]
    x_local = inputs[0]
    scales = inv_rms[0]
    gain_full = gain[0]
    gain_cols = lax.dynamic_slice_in_dim(gain_full, first_col, cols, 0)
    steps = sections + micro - 1

    def step(t, state):
        incoming, grads, stored, gain_accumulator, w_acc, row_store = state
        index = t - section
        active_mask = jnp.logical_and(index >= 0, index < micro)
        slot = jnp.clip(index, 0, micro - 1)
        fresh = lax.dynamic_index_in_dim(cotangent, slot, 0, keepdims=False)
        carry_state = jnp.where(section == 0, fresh, incoming)
        input_row_block = lax.dynamic_index_in_dim(x_local, slot, 0, keepdims=False)
        row_scales_all = lax.dynamic_index_in_dim(scales, slot, 0, keepdims=False)
        down_weight = (
            lax.psum_scatter(
                lax.dot_general(
                    w_local,
                    carry_state,
                    (((1,), (1,)), ((), ())),
                    preferred_element_type=jnp.float32,
                ).astype(jnp.bfloat16),
                "dp",
                scatter_dimension=0,
                tiled=True,
            )
            .astype(jnp.float32)
            .T
        )
        normalized_input = input_row_block.astype(jnp.float32) * row_scales_all[:, None]
        normed_gradient = down_weight * gain_cols[None, :]
        row_statistic = (
            lax.psum(jnp.sum(normed_gradient * normalized_input, axis=1), "dp") / hidden_width
        )
        row_output = row_statistic * root_width / row_scales_all
        result_output = (
            carry_state.astype(jnp.float32)
            + row_scales_all[:, None]
            * (normed_gradient - normalized_input * row_statistic[:, None])
        ).astype(jnp.bfloat16)
        grads = jnp.where(
            active_mask, lax.dynamic_update_index_in_dim(grads, result_output, slot, 0), grads
        )
        stored = jnp.where(
            active_mask, lax.dynamic_update_index_in_dim(stored, carry_state, slot, 0), stored
        )
        row_store = jnp.where(
            active_mask, lax.dynamic_update_index_in_dim(row_store, row_output, slot, 0), row_store
        )
        gain_accumulator = gain_accumulator + jnp.where(
            active_mask, jnp.sum(down_weight * normalized_input, axis=0), 0.0
        )
        incoming = shifted(result_output, "section", 1)
        return (incoming, grads, stored, gain_accumulator, w_acc, row_store)

    start_state = (
        jnp.zeros((rows, cols), jnp.bfloat16),
        jnp.zeros((micro, rows, cols), jnp.bfloat16),
        jnp.zeros((micro, rows, cols), jnp.bfloat16),
        jnp.zeros((cols,), jnp.float32),
        jnp.zeros((hidden_width, cols), jnp.float32),
        jnp.zeros((micro, rows), jnp.float32),
    )
    final = lax.fori_loop(0, steps, step, start_state)
    grads, stored, gain_accumulator, w_acc, row_store = (
        final[1],
        final[2],
        final[3],
        final[4],
        final[5],
    )
    all_rows = x_local.reshape(micro * rows, cols)
    all_scales = scales.reshape(micro * rows)
    all_carry = stored.reshape(micro * rows, cols)
    normed_input = (
        lax.all_gather(all_rows, "dp", axis=1, tiled=True).astype(jnp.float32)
        * all_scales[:, None]
        * gain_full[None, :]
    ).astype(jnp.bfloat16)
    w_acc = lax.dot_general(
        normed_input, all_carry, (((0,), (0,)), ((), ())), preferred_element_type=jnp.float32
    )
    w_acc = w_acc * token_scale
    gain_accumulator = gain_accumulator * token_scale
    return (grads[None], w_acc[None], gain_accumulator[None], row_store[None])


def solution(mesh):
    placed = (
        P(None, None, "dp"),
        P("section", None, None, "dp"),
        P("section", None, None),
        P("section", None),
        P("section", None, "dp"),
    )
    return jax.shard_map(
        body,
        mesh=mesh,
        in_specs=placed,
        out_specs=(
            P("section", None, None, "dp"),
            P("section", None, "dp"),
            P("section", "dp"),
            P("section", None, None),
        ),
        check_vma=False,
    )
```

profile of v0, /device:TPU:23, one launch (start us, length us, event | category | flops | bytes accessed | tf_op | source)
XLA Modules:
  0.0 1308.7 jit_solution(5246431264847894817)
XLA Ops:
  8.8 1230.0 %while.24 = (s32[]{:T(128)}, bf16[128,512]{1,0:T(8,128)(2,1)S(1)}, bf16[2,128,512]{2,1,0:T(8,128)(2,1)S(1)}, bf16[2,128,512]{2,1,0:T(8,128)(2,1)S(1)}, f32[512]{...) while((s32[]{:T(128)}, bf16[128,512]{1,0:T(8,128)(2,1)S(1)}, ...), condition=%wide.region_5.6_spmd.clone, body=%wide.region_0.5_spmd.clone.sunk | while | flops 538772992 | bytes 12214661 | solution.py:86
  14.6 38.4 %reduce-scatter.2.cloned.1.call-done = bf16[512,128]{0,1:T(8,128)(2,1)} async-done(((bf16[4096,128]{0,1:T(8,128)(2,1)}), bf16[512,128]{0,1:T(8,128)(2,1)}) %reduce-scatter.2.cloned.1.call-update) | async-done | bytes 131088 | tf_op jit(solution)/shard_map/while/body/eval_jaxpr/reduce_scatter | solution.py:38
  54.1 14.8 %psum.16 = f32[128]{0:T(128)S(1)} all-reduce(f32[128]{0:T(128)S(1)} %get-tuple-element.463), channel_id=1, replica_groups=mesh['section'=16,'dp'=8] {'dp'}, use_global_device_ids=true, to_apply=%region_3.3 | all-reduce | flops 128 | bytes 1024 | tf_op jit(solution)/shard_map/while/body/eval_jaxpr/psum | solution.py:55
  86.3 39.1 %reduce-scatter.2.cloned.1.call-done = bf16[512,128]{0,1:T(8,128)(2,1)} async-done(((bf16[4096,128]{0,1:T(8,128)(2,1)}), bf16[512,128]{0,1:T(8,128)(2,1)}) %reduce-scatter.2.cloned.1.call-update) | async-done | bytes 131088 | tf_op jit(solution)/shard_map/while/body/eval_jaxpr/reduce_scatter | solution.py:38
  126.5 14.8 %psum.16 = f32[128]{0:T(128)S(1)} all-reduce(f32[128]{0:T(128)S(1)} %get-tuple-element.463), channel_id=1, replica_groups=mesh['section'=16,'dp'=8] {'dp'}, use_global_device_ids=true, to_apply=%region_3.3 | all-reduce | flops 128 | bytes 1024 | tf_op jit(solution)/shard_map/while/body/eval_jaxpr/psum | solution.py:55
  158.7 39.0 %reduce-scatter.2.cloned.1.call-done = bf16[512,128]{0,1:T(8,128)(2,1)} async-done(((bf16[4096,128]{0,1:T(8,128)(2,1)}), bf16[512,128]{0,1:T(8,128)(2,1)}) %reduce-scatter.2.cloned.1.call-update) | async-done | bytes 131088 | tf_op jit(solution)/shard_map/while/body/eval_jaxpr/reduce_scatter | solution.py:38
  231.0 39.2 %reduce-scatter.2.cloned.1.call-done = bf16[512,128]{0,1:T(8,128)(2,1)} async-done(((bf16[4096,128]{0,1:T(8,128)(2,1)}), bf16[512,128]{0,1:T(8,128)(2,1)}) %reduce-scatter.2.cloned.1.call-update) | async-done | bytes 131088 | tf_op jit(solution)/shard_map/while/body/eval_jaxpr/reduce_scatter | solution.py:38
  271.3 14.8 %psum.16 = f32[128]{0:T(128)S(1)} all-reduce(f32[128]{0:T(128)S(1)} %get-tuple-element.463), channel_id=1, replica_groups=mesh['section'=16,'dp'=8] {'dp'}, use_global_device_ids=true, to_apply=%region_3.3 | all-reduce | flops 128 | bytes 1024 | tf_op jit(solution)/shard_map/while/body/eval_jaxpr/psum | solution.py:55
  303.5 39.0 %reduce-scatter.2.cloned.1.call-done = bf16[512,128]{0,1:T(8,128)(2,1)} async-done(((bf16[4096,128]{0,1:T(8,128)(2,1)}), bf16[512,128]{0,1:T(8,128)(2,1)}) %reduce-scatter.2.cloned.1.call-update) | async-done | bytes 131088 | tf_op jit(solution)/shard_map/while/body/eval_jaxpr/reduce_scatter | solution.py:38
  343.7 14.8 %psum.16 = f32[128]{0:T(128)S(1)} all-reduce(f32[128]{0:T(128)S(1)} %get-tuple-element.463), channel_id=1, replica_groups=mesh['section'=16,'dp'=8] {'dp'}, use_global_device_ids=true, to_apply=%region_3.3 | all-reduce | flops 128 | bytes 1024 | tf_op jit(solution)/shard_map/while/body/eval_jaxpr/psum | solution.py:55
  375.8 39.0 %reduce-scatter.2.cloned.1.call-done = bf16[512,128]{0,1:T(8,128)(2,1)} async-done(((bf16[4096,128]{0,1:T(8,128)(2,1)}), bf16[512,128]{0,1:T(8,128)(2,1)}) %reduce-scatter.2.cloned.1.call-update) | async-done | bytes 131088 | tf_op jit(solution)/shard_map/while/body/eval_jaxpr/reduce_scatter | solution.py:38
  448.1 39.0 %reduce-scatter.2.cloned.1.call-done = bf16[512,128]{0,1:T(8,128)(2,1)} async-done(((bf16[4096,128]{0,1:T(8,128)(2,1)}), bf16[512,128]{0,1:T(8,128)(2,1)}) %reduce-scatter.2.cloned.1.call-update) | async-done | bytes 131088 | tf_op jit(solution)/shard_map/while/body/eval_jaxpr/reduce_scatter | solution.py:38
  488.2 14.9 %psum.16 = f32[128]{0:T(128)S(1)} all-reduce(f32[128]{0:T(128)S(1)} %get-tuple-element.463), channel_id=1, replica_groups=mesh['section'=16,'dp'=8] {'dp'}, use_global_device_ids=true, to_apply=%region_3.3 | all-reduce | flops 128 | bytes 1024 | tf_op jit(solution)/shard_map/while/body/eval_jaxpr/psum | solution.py:55
  520.4 39.1 %reduce-scatter.2.cloned.1.call-done = bf16[512,128]{0,1:T(8,128)(2,1)} async-done(((bf16[4096,128]{0,1:T(8,128)(2,1)}), bf16[512,128]{0,1:T(8,128)(2,1)}) %reduce-scatter.2.cloned.1.call-update) | async-done | bytes 131088 | tf_op jit(solution)/shard_map/while/body/eval_jaxpr/reduce_scatter | solution.py:38
  592.9 39.1 %reduce-scatter.2.cloned.1.call-done = bf16[512,128]{0,1:T(8,128)(2,1)} async-done(((bf16[4096,128]{0,1:T(8,128)(2,1)}), bf16[512,128]{0,1:T(8,128)(2,1)}) %reduce-scatter.2.cloned.1.call-update) | async-done | bytes 131088 | tf_op jit(solution)/shard_map/while/body/eval_jaxpr/reduce_scatter | solution.py:38
  633.1 14.8 %psum.16 = f32[128]{0:T(128)S(1)} all-reduce(f32[128]{0:T(128)S(1)} %get-tuple-element.463), channel_id=1, replica_groups=mesh['section'=16,'dp'=8] {'dp'}, use_global_device_ids=true, to_apply=%region_3.3 | all-reduce | flops 128 | bytes 1024 | tf_op jit(solution)/shard_map/while/body/eval_jaxpr/psum | solution.py:55
  665.3 39.1 %reduce-scatter.2.cloned.1.call-done = bf16[512,128]{0,1:T(8,128)(2,1)} async-done(((bf16[4096,128]{0,1:T(8,128)(2,1)}), bf16[512,128]{0,1:T(8,128)(2,1)}) %reduce-scatter.2.cloned.1.call-update) | async-done | bytes 131088 | tf_op jit(solution)/shard_map/while/body/eval_jaxpr/reduce_scatter | solution.py:38
  705.5 14.4 %psum.16 = f32[128]{0:T(128)S(1)} all-reduce(f32[128]{0:T(128)S(1)} %get-tuple-element.463), channel_id=1, replica_groups=mesh['section'=16,'dp'=8] {'dp'}, use_global_device_ids=true, to_apply=%region_3.3 | all-reduce | flops 128 | bytes 1024 | tf_op jit(solution)/shard_map/while/body/eval_jaxpr/psum | solution.py:55
  737.7 39.1 %reduce-scatter.2.cloned.1.call-done = bf16[512,128]{0,1:T(8,128)(2,1)} async-done(((bf16[4096,128]{0,1:T(8,128)(2,1)}), bf16[512,128]{0,1:T(8,128)(2,1)}) %reduce-scatter.2.cloned.1.call-update) | async-done | bytes 131088 | tf_op jit(solution)/shard_map/while/body/eval_jaxpr/reduce_scatter | solution.py:38
  777.9 14.8 %psum.16 = f32[128]{0:T(128)S(1)} all-reduce(f32[128]{0:T(128)S(1)} %get-tuple-element.463), channel_id=1, replica_groups=mesh['section'=16,'dp'=8] {'dp'}, use_global_device_ids=true, to_apply=%region_3.3 | all-reduce | flops 128 | bytes 1024 | tf_op jit(solution)/shard_map/while/body/eval_jaxpr/psum | solution.py:55
  810.1 39.2 %reduce-scatter.2.cloned.1.call-done = bf16[512,128]{0,1:T(8,128)(2,1)} async-done(((bf16[4096,128]{0,1:T(8,128)(2,1)}), bf16[512,128]{0,1:T(8,128)(2,1)}) %reduce-scatter.2.cloned.1.call-update) | async-done | bytes 131088 | tf_op jit(solution)/shard_map/while/body/eval_jaxpr/reduce_scatter | solution.py:38
  850.4 14.8 %psum.16 = f32[128]{0:T(128)S(1)} all-reduce(f32[128]{0:T(128)S(1)} %get-tuple-element.463), channel_id=1, replica_groups=mesh['section'=16,'dp'=8] {'dp'}, use_global_device_ids=true, to_apply=%region_3.3 | all-reduce | flops 128 | bytes 1024 | tf_op jit(solution)/shard_map/while/body/eval_jaxpr/psum | solution.py:55
  882.6 39.1 %reduce-scatter.2.cloned.1.call-done = bf16[512,128]{0,1:T(8,128)(2,1)} async-done(((bf16[4096,128]{0,1:T(8,128)(2,1)}), bf16[512,128]{0,1:T(8,128)(2,1)}) %reduce-scatter.2.cloned.1.call-update) | async-done | bytes 131088 | tf_op jit(solution)/shard_map/while/body/eval_jaxpr/reduce_scatter | solution.py:38
  922.8 14.8 %psum.16 = f32[128]{0:T(128)S(1)} all-reduce(f32[128]{0:T(128)S(1)} %get-tuple-element.463), channel_id=1, replica_groups=mesh['section'=16,'dp'=8] {'dp'}, use_global_device_ids=true, to_apply=%region_3.3 | all-reduce | flops 128 | bytes 1024 | tf_op jit(solution)/shard_map/while/body/eval_jaxpr/psum | solution.py:55
  955.0 38.9 %reduce-scatter.2.cloned.1.call-done = bf16[512,128]{0,1:T(8,128)(2,1)} async-done(((bf16[4096,128]{0,1:T(8,128)(2,1)}), bf16[512,128]{0,1:T(8,128)(2,1)}) %reduce-scatter.2.cloned.1.call-update) | async-done | bytes 131088 | tf_op jit(solution)/shard_map/while/body/eval_jaxpr/reduce_scatter | solution.py:38
  1027.2 39.3 %reduce-scatter.2.cloned.1.call-done = bf16[512,128]{0,1:T(8,128)(2,1)} async-done(((bf16[4096,128]{0,1:T(8,128)(2,1)}), bf16[512,128]{0,1:T(8,128)(2,1)}) %reduce-scatter.2.cloned.1.call-update) | async-done | bytes 131088 | tf_op jit(solution)/shard_map/while/body/eval_jaxpr/reduce_scatter | solution.py:38
  1067.7 14.9 %psum.16 = f32[128]{0:T(128)S(1)} all-reduce(f32[128]{0:T(128)S(1)} %get-tuple-element.463), channel_id=1, replica_groups=mesh['section'=16,'dp'=8] {'dp'}, use_global_device_ids=true, to_apply=%region_3.3 | all-reduce | flops 128 | bytes 1024 | tf_op jit(solution)/shard_map/while/body/eval_jaxpr/psum | solution.py:55
  1099.9 39.0 %reduce-scatter.2.cloned.1.call-done = bf16[512,128]{0,1:T(8,128)(2,1)} async-done(((bf16[4096,128]{0,1:T(8,128)(2,1)}), bf16[512,128]{0,1:T(8,128)(2,1)}) %reduce-scatter.2.cloned.1.call-update) | async-done | bytes 131088 | tf_op jit(solution)/shard_map/while/body/eval_jaxpr/reduce_scatter | solution.py:38
  1140.0 14.8 %psum.16 = f32[128]{0:T(128)S(1)} all-reduce(f32[128]{0:T(128)S(1)} %get-tuple-element.463), channel_id=1, replica_groups=mesh['section'=16,'dp'=8] {'dp'}, use_global_device_ids=true, to_apply=%region_3.3 | all-reduce | flops 128 | bytes 1024 | tf_op jit(solution)/shard_map/while/body/eval_jaxpr/psum | solution.py:55
  1172.1 39.0 %reduce-scatter.2.cloned.1.call-done = bf16[512,128]{0,1:T(8,128)(2,1)} async-done(((bf16[4096,128]{0,1:T(8,128)(2,1)}), bf16[512,128]{0,1:T(8,128)(2,1)}) %reduce-scatter.2.cloned.1.call-update) | async-done | bytes 131088 | tf_op jit(solution)/shard_map/while/body/eval_jaxpr/reduce_scatter | solution.py:38
  1212.3 14.8 %psum.16 = f32[128]{0:T(128)S(1)} all-reduce(f32[128]{0:T(128)S(1)} %get-tuple-element.463), channel_id=1, replica_groups=mesh['section'=16,'dp'=8] {'dp'}, use_global_device_ids=true, to_apply=%region_3.3 | all-reduce | flops 128 | bytes 1024 | tf_op jit(solution)/shard_map/while/body/eval_jaxpr/psum | solution.py:55
  1239.9 55.1 %all-gather.2.cloned.1.call-done = bf16[256,4096]{1,0:T(8,128)(2,1)} async-done(((bf16[256,512]{1,0:T(8,128)(2,1)}), bf16[256,4096]{1,0:T(8,128)(2,1)}) %all-gather.2.cloned.1.call-update) | async-done | bytes 2097168 | tf_op jit(solution)/shard_map/all_gather | solution.py:98
  (309 shorter events, 381.2 us)
Async XLA Ops:
  8.8 44.2 %reduce-scatter.2.cloned.1.call-start = ((), (), s32[]{:S(2)}) async-start(), calls=%async_computation.2 | async-start | bytes 1179648 | tf_op jit(solution)/shard_map/while/body/eval_jaxpr/reduce_scatter | solution.py:38
  70.1 10.5 collective-permute-start
  80.6 44.8 %reduce-scatter.2.cloned.1.call-start = ((), (), s32[]{:S(2)}) async-start(), calls=%async_computation.2 | async-start | bytes 1179648 | tf_op jit(solution)/shard_map/while/body/eval_jaxpr/reduce_scatter | solution.py:38
  142.5 10.5 collective-permute-start
  153.0 44.7 %reduce-scatter.2.cloned.1.call-start = ((), (), s32[]{:S(2)}) async-start(), calls=%async_computation.2 | async-start | bytes 1179648 | tf_op jit(solution)/shard_map/while/body/eval_jaxpr/reduce_scatter | solution.py:38
  214.2 11.1 collective-permute-start
  225.3 44.9 %reduce-scatter.2.cloned.1.call-start = ((), (), s32[]{:S(2)}) async-start(), calls=%async_computation.2 | async-start | bytes 1179648 | tf_op jit(solution)/shard_map/while/body/eval_jaxpr/reduce_scatter | solution.py:38
  297.8 44.7 %reduce-scatter.2.cloned.1.call-start = ((), (), s32[]{:S(2)}) async-start(), calls=%async_computation.2 | async-start | bytes 1179648 | tf_op jit(solution)/shard_map/while/body/eval_jaxpr/reduce_scatter | solution.py:38
  359.7 10.5 collective-permute-start
  370.1 44.7 %reduce-scatter.2.cloned.1.call-start = ((), (), s32[]{:S(2)}) async-start(), calls=%async_computation.2 | async-start | bytes 1179648 | tf_op jit(solution)/shard_map/while/body/eval_jaxpr/reduce_scatter | solution.py:38
  431.3 11.1 collective-permute-start
  442.4 44.7 %reduce-scatter.2.cloned.1.call-start = ((), (), s32[]{:S(2)}) async-start(), calls=%async_computation.2 | async-start | bytes 1179648 | tf_op jit(solution)/shard_map/while/body/eval_jaxpr/reduce_scatter | solution.py:38
  504.2 10.5 collective-permute-start
  514.7 44.8 %reduce-scatter.2.cloned.1.call-start = ((), (), s32[]{:S(2)}) async-start(), calls=%async_computation.2 | async-start | bytes 1179648 | tf_op jit(solution)/shard_map/while/body/eval_jaxpr/reduce_scatter | solution.py:38
  576.0 11.2 collective-permute-start
  587.2 44.8 %reduce-scatter.2.cloned.1.call-start = ((), (), s32[]{:S(2)}) async-start(), calls=%async_computation.2 | async-start | bytes 1179648 | tf_op jit(solution)/shard_map/while/body/eval_jaxpr/reduce_scatter | solution.py:38
  659.6 44.8 %reduce-scatter.2.cloned.1.call-start = ((), (), s32[]{:S(2)}) async-start(), calls=%async_computation.2 | async-start | bytes 1179648 | tf_op jit(solution)/shard_map/while/body/eval_jaxpr/reduce_scatter | solution.py:38
  721.0 10.9 collective-permute-start
  732.0 44.8 %reduce-scatter.2.cloned.1.call-start = ((), (), s32[]{:S(2)}) async-start(), calls=%async_computation.2 | async-start | bytes 1179648 | tf_op jit(solution)/shard_map/while/body/eval_jaxpr/reduce_scatter | solution.py:38
  793.9 10.5 collective-permute-start
  804.4 44.9 %reduce-scatter.2.cloned.1.call-start = ((), (), s32[]{:S(2)}) async-start(), calls=%async_computation.2 | async-start | bytes 1179648 | tf_op jit(solution)/shard_map/while/body/eval_jaxpr/reduce_scatter | solution.py:38
  866.4 10.5 collective-permute-start
  876.9 44.8 %reduce-scatter.2.cloned.1.call-start = ((), (), s32[]{:S(2)}) async-start(), calls=%async_computation.2 | async-start | bytes 1179648 | tf_op jit(solution)/shard_map/while/body/eval_jaxpr/reduce_scatter | solution.py:38
  938.8 10.5 collective-permute-start
  949.3 44.6 %reduce-scatter.2.cloned.1.call-start = ((), (), s32[]{:S(2)}) async-start(), calls=%async_computation.2 | async-start | bytes 1179648 | tf_op jit(solution)/shard_map/while/body/eval_jaxpr/reduce_scatter | solution.py:38
  1010.5 11.0 collective-permute-start
  1021.5 45.0 %reduce-scatter.2.cloned.1.call-start = ((), (), s32[]{:S(2)}) async-start(), calls=%async_computation.2 | async-start | bytes 1179648 | tf_op jit(solution)/shard_map/while/body/eval_jaxpr/reduce_scatter | solution.py:38
  1083.7 10.5 collective-permute-start
  1094.2 44.7 %reduce-scatter.2.cloned.1.call-start = ((), (), s32[]{:S(2)}) async-start(), calls=%async_computation.2 | async-start | bytes 1179648 | tf_op jit(solution)/shard_map/while/body/eval_jaxpr/reduce_scatter | solution.py:38
  1155.9 10.5 collective-permute-start
  1166.4 44.7 %reduce-scatter.2.cloned.1.call-start = ((), (), s32[]{:S(2)}) async-start(), calls=%async_computation.2 | async-start | bytes 1179648 | tf_op jit(solution)/shard_map/while/body/eval_jaxpr/reduce_scatter | solution.py:38
  1238.8 56.3 %all-gather.2.cloned.1.call-start = ((), (), s32[]{:S(2)}) async-start(), calls=%async_computation.1 | async-start | bytes 2359296 | tf_op jit(solution)/shard_map/all_gather | solution.py:98
  (40 other events, 2300.9 us)
Sparse Core Ops, SparseCore 0:
  14.7 38.2 reduce-scatter.1
  86.4 38.9 reduce-scatter.1
  158.8 38.8 reduce-scatter.1
  231.1 39.0 reduce-scatter.1
  303.6 38.9 reduce-scatter.1
  375.9 38.8 reduce-scatter.1
  448.2 38.8 reduce-scatter.1
  520.5 38.9 reduce-scatter.1
  593.0 38.9 reduce-scatter.1
  665.4 38.9 reduce-scatter.1
  737.8 38.9 reduce-scatter.1
  810.2 39.0 reduce-scatter.1
  882.7 38.9 reduce-scatter.1
  955.1 38.7 reduce-scatter.1
  1027.3 39.1 reduce-scatter.1
  1100.0 38.8 reduce-scatter.1
  1172.2 38.9 reduce-scatter.1
Sparse Core Ops, SparseCore 1:
  1240.9 54.1 all-gather.1
where the time goes:
time: 1310 us
  waiting for transfers between devices  878 us (67%)
  blocking collectives  249 us (19%)
  matrix products  85.4 us (7%)
  other arithmetic  55.5 us (4%)
  starting transfers between devices  22 us (2%)
  between operations  15.2 us (1%)
    reduce_scatter x17, waiting for transfers between devices, step(): lax.psum_scatter(lax.dot_general(w_local, carry_state, (((1,), (1,)), (()...  664 us
    psum x17, blocking collectives, step(): lax.psum(jnp.sum(normed_gradient * normalized_input, axis=1), 'dp')  249 us
    ppermute x17, waiting for transfers between devices, shifted(): return lax.ppermute(block, axis, route)  159 us
    dot_general x17, matrix products, step(): lax.dot_general(w_local, carry_state, (((1,), (1,)), ((), ())), preferred...  78.9 us
    all_gather x1, waiting for transfers between devices, body(): lax.all_gather(all_rows, 'dp', axis=1, tiled=True).astype(jnp.float32)  55.1 us
  transfers between devices with their start and end apart: 35, of which 35 were waited for; matrix products, arithmetic and copies ran while one was open for 0% of the time, Pallas kernels for 0%

commit v1 on v0

v1 whole, which is shorter than its diff:
```python
import functools

import jax
import jax.numpy as jnp
from jax import lax
from jax.experimental import pallas as pl
from jax.experimental.pallas import tpu as pltpu
from jax.sharding import PartitionSpec as P

MESH = pl.DeviceIdType.MESH
F32 = jnp.float32
BF16 = jnp.bfloat16
CHUNK = 16
GROUP = 64
FAR_FIRST = (5, 4, 3, 7, 2, 6, 1)
LAG = 3


def wide(block, times):
    return jnp.concatenate([block] * times, axis=1)


def chain_kernel(
    sections, n_dp, rows, cols,
    cot_ref, x_ref, r_ref, gain_ref, w_hbm,
    carry, gout, ggrad, rdot, normed_hbm,
    w, wt, xg, normed, u, xprev, rb, sb, rq, qbuf, g1, g1r, stat, statr,
    w_sem, xg_send, xg_recv, xp_send, xp_recv, rq_recv, q_send, back_send, back_recv,
    g1_send, g1_recv, st_send, st_recv, n_sem,
):
    s, d = lax.axis_index("section"), lax.axis_index("dp")
    last = sections - 1
    chunks, groups = rows // CHUNK, rows // GROUP
    width = n_dp * cols
    nxt = jnp.minimum(s + 1, last)
    prev = jnp.maximum(s - 1, 0)
    lanes = rb.shape[1]

    def peer(i):
        return (d + i) % n_dp

    def w_copy(k):
        part = pl.ds(pl.multiple_of(k * cols, cols), cols)
        return pltpu.make_async_copy(w_hbm.at[part, :], w.at[part, :], w_sem.at[k])

    @pl.loop(0, n_dp)
    def _(k):
        w_copy(k).start()

    barrier = pltpu.get_barrier_semaphore()

    @pl.loop(1, n_dp)
    def _(i):
        pl.semaphore_signal(barrier, inc=1, device_id=(s, peer(i)), device_id_type=MESH)

    @pl.when(s > 0)
    def _():
        @pl.loop(0, n_dp)
        def _(i):
            pl.semaphore_signal(barrier, inc=1, device_id=(prev, i), device_id_type=MESH)

    @pl.when(s < last)
    def _():
        @pl.loop(0, n_dp)
        def _(i):
            pl.semaphore_signal(barrier, inc=1, device_id=(nxt, i), device_id_type=MESH)

    for m in range(rows // lanes):
        rb[pl.ds(m * lanes, lanes), :] = jnp.broadcast_to(r_ref[pl.ds(m, 1), :], (lanes, lanes)).T
    g1[...] = jnp.zeros_like(g1)

    @pl.when(s == last)
    def _():
        g1r[...] = jnp.zeros_like(g1r)

    inner = jnp.logical_and(s > 0, s < last)
    pl.semaphore_wait(barrier, jnp.where(inner, 3 * n_dp - 1, 2 * n_dp - 1))

    def group_rows(g):
        return pl.ds(pl.multiple_of(g * GROUP, GROUP), GROUP)

    @pl.loop(0, groups)
    def _(g):
        part = group_rows(g)
        pltpu.make_async_copy(x_ref.at[part, :], xg.at[d, part, :], xg_recv.at[g]).start()

        @pl.loop(1, n_dp)
        def _(i):
            pltpu.make_async_remote_copy(
                x_ref.at[part, :], xg.at[d, part, :], xg_send, xg_recv.at[g],
                device_id=(s, peer(i)), device_id_type=MESH,
            ).start()

    @pl.when(s < last)
    def _():
        pltpu.make_async_remote_copy(
            x_ref, xprev, xp_send, xp_recv, device_id=(nxt, d), device_id_type=MESH
        ).start()

    @pl.loop(0, n_dp)
    def _(k):
        w_copy(k).wait()
        part = pl.ds(pl.multiple_of(k * cols, cols), cols)
        wt[:, part] = w[part, :].T

    def project(g):
        part = group_rows(g)
        pltpu.make_async_copy(xg.at[:, part, :], xg.at[:, part, :], xg_recv.at[g]).wait()
        scale = wide(rb[part, :], cols // lanes)

        @pl.loop(0, n_dp)
        def _(k):
            block = pl.ds(pl.multiple_of(k * cols, cols), cols)
            normed[part, block] = (
                xg[k, part, :].astype(F32) * scale * gain_ref[:, block]
            ).astype(BF16)

        pltpu.make_async_copy(normed.at[part, :], normed_hbm.at[part, :], n_sem.at[g]).start()
        u[part, :] = jnp.dot(normed[part, :], w[...], preferred_element_type=F32)

    early = jnp.where(s < 6, 1, groups)

    @pl.loop(0, early)
    def _(g):
        project(g)

    def chunk_rows(i):
        return pl.ds(pl.multiple_of(i * CHUNK, CHUNK), CHUNK)

    def total(slot):
        pltpu.make_async_copy(rq.at[slot], rq.at[slot], rq_recv.at[slot]).wait()
        added = rq[slot, 0].astype(F32)
        for k in range(1, n_dp):
            added += rq[slot, k].astype(F32)
        return added, (rq[slot, n_dp].astype(F32) + added).astype(BF16)

    def add_gain(where, x_rows, added):
        term = x_rows.astype(F32) * added
        for b in range(CHUNK // 8):
            where[...] += term[b * 8 : (b + 1) * 8, :]

    def finish(i):
        part = chunk_rows(i)
        added, result = total(chunks + i)
        gout[part, :] = result
        add_gain(g1r, x_ref[part, :], added)

    @pl.when(s > 0)
    def _():
        pltpu.make_async_copy(xprev, xprev, xp_recv).wait()

    @pl.loop(0, chunks)
    def _(i):
        part = chunk_rows(i)

        @pl.when(s == 0)
        def _():
            carry[part, :] = cot_ref[part, :]

        @pl.when(s > 0)
        def _():
            added, result = total(i)
            carry[part, :] = result
            pltpu.make_async_remote_copy(
                carry.at[part, :], gout.at[part, :], back_send, back_recv,
                device_id=(prev, d), device_id_type=MESH,
            ).start()
            add_gain(g1, xprev[part, :], added)

        slot = jnp.where(s == last, chunks + i, i)

        @pl.when(s < last)
        def _():
            pltpu.make_async_remote_copy(
                carry.at[part, :], rq.at[slot, n_dp], q_send, rq_recv.at[slot],
                device_id=(nxt, d), device_id_type=MESH,
            ).start()

        @pl.when(s == last)
        def _():
            pltpu.make_async_copy(carry.at[part, :], rq.at[slot, n_dp], rq_recv.at[slot]).start()

        mine = carry[part, :]
        scale = rb[part, :]
        dots = mine.astype(F32) * u[part, :]
        row = jnp.sum(dots, axis=1, keepdims=True) * (1.0 / width)
        row = jnp.broadcast_to(row, (CHUNK, lanes))
        sb[part, :] = row
        shift = wide(row * scale * scale, cols // lanes)
        scale = wide(scale, cols // lanes)

        def sums(f):
            block = pl.ds(pl.multiple_of(f * cols, cols), cols)
            product = jnp.dot(mine, wt[:, block], preferred_element_type=F32)
            qbuf[i, f] = (
                product * scale * gain_ref[:, block] - xg[f, part, :].astype(F32) * shift
            ).astype(BF16)

        for off in FAR_FIRST:
            f = d + off - 2 * sum(((d // b) % 2) * b for b in (1, 2, 4) if off & b)
            sums(f)
            pltpu.make_async_remote_copy(
                qbuf.at[i, f], rq.at[slot, d], q_send, rq_recv.at[slot],
                device_id=(nxt, f), device_id_type=MESH,
            ).start()
        sums(d)

        @pl.when(s < last)
        def _():
            pltpu.make_async_remote_copy(
                qbuf.at[i, d], rq.at[slot, d], q_send, rq_recv.at[slot],
                device_id=(nxt, d), device_id_type=MESH,
            ).start()

        @pl.when(s == last)
        def _():
            pltpu.make_async_copy(qbuf.at[i, d], rq.at[slot, d], rq_recv.at[slot]).start()

        per = GROUP // CHUNK

        @pl.when(jnp.logical_and(early == 1, jnp.logical_and(i % per == per // 2, i // per + 1 < groups)))
        def _():
            project(i // per + 1)

        @pl.when(jnp.logical_and(s == last, i >= LAG))
        def _():
            finish(i - LAG)

    stat[...] = jnp.zeros_like(stat)
    for m in range(rows // lanes):
        turned = sb[pl.ds(m * lanes, lanes), :].T
        stat[pl.ds(m, 1), :] = turned[0:1, :]

    pltpu.make_async_copy(stat, statr.at[d], st_recv).start()

    @pl.loop(1, n_dp)
    def _(i):
        pltpu.make_async_remote_copy(
            stat, statr.at[d], st_send, st_recv, device_id=(s, peer(i)), device_id_type=MESH
        ).start()

    @pl.when(s > 0)
    def _():
        pltpu.make_async_remote_copy(
            g1, g1r, g1_send, g1_recv, device_id=(prev, d), device_id_type=MESH
        ).start()
        pltpu.make_async_copy(g1, g1, g1_send).wait()

    @pl.when(s == last)
    def _():
        @pl.loop(chunks - LAG, chunks)
        def _(i):
            finish(i)

    pltpu.make_async_copy(statr, statr, st_recv).wait()
    rows_stat = statr[0]
    for k in range(1, n_dp):
        rows_stat += statr[k]
    halves = rows // lanes
    rdot[...] = rows_stat[:halves, :] * (float(width) ** 0.5) / r_ref[...]

    own = pl.ds(pl.multiple_of(d * cols, cols), cols)
    second = jnp.zeros((8, cols), F32)
    for m in range(halves):
        part = pl.ds(m * lanes, lanes)
        column = jnp.broadcast_to(rows_stat[m : m + 1, :], (lanes, lanes)).T
        factor = column * rb[part, :] * rb[part, :]
        block = x_ref[part, :].astype(F32)
        term = block * block * wide(factor, cols // lanes)
        second += jnp.sum(term.reshape(lanes // 8, 8, cols), axis=0)

    @pl.when(s < last)
    def _():
        pltpu.make_async_copy(g1r, g1r, g1_recv).wait()
        pltpu.make_async_copy(gout, gout, back_recv).wait()

    ggrad[...] = (
        jnp.sum(second + g1r[...], axis=0, keepdims=True)
        * (float(rows) ** -0.5)
        / gain_ref[:, own]
    )

    def sent(amount, semaphore):
        pltpu.make_async_copy(amount, amount, semaphore).wait()

    sent(xg.at[pl.ds(0, n_dp - 1)], xg_send)
    sent(statr.at[pl.ds(0, n_dp - 1)], st_send)

    @pl.when(s < last)
    def _():
        sent(x_ref, xp_send)
        sent(rq.at[pl.ds(0, chunks)], q_send)

    @pl.when(s == last)
    def _():
        sent(qbuf.at[:, pl.ds(0, n_dp - 1)], q_send)

    @pl.when(s > 0)
    def _():
        sent(carry, back_send)

    @pl.loop(0, groups)
    def _(g):
        part = group_rows(g)
        pltpu.make_async_copy(normed.at[part, :], normed_hbm.at[part, :], n_sem.at[g]).wait()


def chain(n_sec, n_dp, cotangent, x, scales, gain, weight):
    rows, cols = x.shape
    width = n_dp * cols
    lanes = scales.shape[1]
    chunks, groups = rows // CHUNK, rows // GROUP
    vmem = pl.BlockSpec(memory_space=pltpu.VMEM)
    hbm = pl.BlockSpec(memory_space=pl.ANY)
    sem = pltpu.SemaphoreType.DMA
    return pl.pallas_call(
        functools.partial(chain_kernel, n_sec, n_dp, rows, cols),
        name="chain",
        out_shape=(
            jax.ShapeDtypeStruct((rows, cols), BF16),
            jax.ShapeDtypeStruct((rows, cols), BF16),
            jax.ShapeDtypeStruct((1, cols), F32),
            jax.ShapeDtypeStruct(scales.shape, F32),
            jax.ShapeDtypeStruct((rows, width), BF16),
        ),
        in_specs=[vmem, vmem, vmem, vmem, hbm],
        out_specs=(vmem, vmem, vmem, vmem, hbm),
        scratch_shapes=[
            pltpu.VMEM((width, cols), BF16),
            pltpu.VMEM((cols, width), BF16),
            pltpu.VMEM((n_dp, rows, cols), BF16),
            pltpu.VMEM((rows, width), BF16),
            pltpu.VMEM((rows, cols), F32),
            pltpu.VMEM((rows, cols), BF16),
            pltpu.VMEM((rows, lanes), F32),
            pltpu.VMEM((rows, lanes), F32),
            pltpu.VMEM((2 * chunks, n_dp + 1, CHUNK, cols), BF16),
            pltpu.VMEM((chunks, n_dp, CHUNK, cols), BF16),
            pltpu.VMEM((8, cols), F32),
            pltpu.VMEM((8, cols), F32),
            pltpu.VMEM((8, lanes), F32),
            pltpu.VMEM((n_dp, 8, lanes), F32),
            sem((n_dp,)), sem, sem((groups,)), sem, sem, sem((2 * chunks,)), sem, sem, sem,
            sem, sem, sem, sem, sem((groups,)),
        ],
        compiler_params=pltpu.CompilerParams(
            collective_id=0, has_side_effects=True, vmem_limit_bytes=48 << 20
        ),
    )(cotangent, x, scales, gain, weight)


def weight_kernel(scale, normed, carry, grads, gain_grad, row_dot, w_out, g_out, gg_out, rd_out):
    w_out[...] = scale * lax.dot_general(
        normed[...], carry[...], (((0,), (0,)), ((), ())), preferred_element_type=F32
    )

    @pl.when(pl.program_id(0) == 0)
    def _():
        g_out[...] = grads[...]
        gg_out[...] = gain_grad[...]
        rd_out[...] = row_dot[...]


def weight_grads(normed, carry, grads, gain_grad, row_dot):
    rows, width = normed.shape
    cols = carry.shape[1]
    whole = lambda a: pl.BlockSpec(a.shape, lambda k: (0, 0))
    return pl.pallas_call(
        functools.partial(weight_kernel, float(rows) ** -0.5),
        name="weight_grads",
        grid=(width // cols,),
        out_shape=(
            jax.ShapeDtypeStruct((width, cols), F32),
            jax.ShapeDtypeStruct(grads.shape, grads.dtype),
            jax.ShapeDtypeStruct(gain_grad.shape, F32),
            jax.ShapeDtypeStruct(row_dot.shape, F32),
        ),
        in_specs=[
            pl.BlockSpec((rows, cols), lambda k: (0, k)),
            whole(carry), whole(grads), whole(gain_grad), whole(row_dot),
        ],
        out_specs=(
            pl.BlockSpec((cols, cols), lambda k: (k, 0)),
            whole(grads), whole(gain_grad), whole(row_dot),
        ),
        compiler_params=pltpu.CompilerParams(vmem_limit_bytes=24 << 20),
    )(normed, carry, grads, gain_grad, row_dot)


def body(n_sec, n_dp, cotangent, inputs, inv_rms, gain, weight):
    micro, per, cols = cotangent.shape
    rows = micro * per
    carry, grads, gain_grad, row_dot, normed = chain(
        n_sec, n_dp, cotangent.reshape(rows, cols), inputs.reshape(rows, cols),
        inv_rms[0], gain, weight[0],
    )
    w_grad, grads, gain_grad, row_dot = weight_grads(normed, carry, grads, gain_grad, row_dot)
    return grads.reshape(1, micro, per, cols), w_grad[None], gain_grad, row_dot[None]


def solution(mesh):
    return jax.shard_map(
        functools.partial(body, mesh.shape["section"], mesh.shape["dp"]),
        mesh=mesh,
        in_specs=(
            P(None, None, "dp"),
            P("section", None, None, "dp"),
            P("section", None, None),
            P("section", None),
            P("section", None, "dp"),
        ),
        out_specs=(
            P("section", None, None, "dp"),
            P("section", None, "dp"),
            P("section", "dp"),
            P("section", None, None),
        ),
        check_vma=False,
    )
```

time: 1310 us -> 149 us (0.11)
  waiting for transfers between devices: 878 us -> 0 us
  blocking collectives: 249 us -> 0 us
  Pallas kernels: 0 us -> 145 us
  matrix products: 85.4 us -> 0 us
  other arithmetic: 55.5 us -> 0 us
  starting transfers between devices: 22 us -> 0 us
  between operations: 15.2 us -> 0.65 us
    reduce_scatter x17 -> x0, waiting for transfers between devices: 664 us -> none  [step(): lax.psum_scatter(lax.dot_general(w_local, carry_state, (((1,), (1,)), (()...]
    psum x17 -> x0, blocking collectives: 249 us -> none  [step(): lax.psum(jnp.sum(normed_gradient * normalized_input, axis=1), 'dp')]
    ppermute x17 -> x0, waiting for transfers between devices: 159 us -> none  [shifted(): return lax.ppermute(block, axis, route)]
    pallas_call x0 -> x2, Pallas kernels: none -> 145 us  [the longest x1 139 us: chain(): pl.pallas_call(functools.partial(chain_kernel, n_sec, n_dp, rows, cols),...]
    dot_general x18 -> x0, matrix products: 85.4 us -> none  [the longest x17 78.9 us: step(): lax.dot_general(w_local, carry_state, (((1,), (1,)), ((), ())), preferred...]
    all_gather x1 -> x0, waiting for transfers between devices: 55.1 us -> none  [body(): lax.all_gather(all_rows, 'dp', axis=1, tiled=True).astype(jnp.float32)]
    select_n x51 -> x0, other arithmetic: 35.7 us -> none  [the longest x17 18.5 us: step(): jnp.where(active_mask, lax.dynamic_update_index_in_dim(grads, result_outp...]
    ppermute x17 -> x0, starting transfers between devices: 22 us -> none  [shifted(): return lax.ppermute(block, axis, route)]
  transfers between devices with their start and end apart: 35 -> 0, of which waited for: 35 -> 0; matrix products, arithmetic and copies ran while one was open for 0% -> 0% of each run, Pallas kernels for 0% -> 0%
where the time goes in v1:
time: 149 us
  Pallas kernels  145 us (97%)
  local copies, waits for them, and re-layouts  3.29 us (2%)
    pallas_call x1, Pallas kernels, chain(): pl.pallas_call(functools.partial(chain_kernel, n_sec, n_dp, rows, cols),...  139 us
    pallas_call x1, Pallas kernels, weight_grads(): pl.pallas_call(functools.partial(weight_kernel, float(rows) ** (-0.5)), n...  5.76 us
    unnamed x8, local copies, waits for them, and re-layouts  3.29 us

profile of v1, /device:TPU:23, one launch (start us, length us, event | category | flops | bytes accessed | tf_op | source)
XLA Modules:
  0.0 148.6 jit_solution(3670471205532082330)
XLA Ops:
  0.6 0.0 copy-start
  0.6 0.9 copy-done
  1.6 0.0 copy-start.1
  1.6 0.9 copy-done.1
  2.5 0.0 copy-start.2
  2.5 0.7 copy-done.2
  3.3 0.0 copy-start.3
  3.3 0.7 copy-done.3
  3.9 138.9 %chain.1 = (bf16[256,512]{1,0:T(8,128)(2,1)S(1)}, bf16[256,512]{1,0:T(8,128)(2,1)S(1)}, f32[1,512]{1,0:T(1,128)S(1)}, f32[2,128]{1,0:T(2,128)S(1)}, bf16[256,4096]{1,0:T(8,128)(2,1)S(1)}) custom-call(bf16[256,512]{1,0:T(8,128)(2,1)S(1)} %bitcast.7, bf16[256,512]{1,0:T(8,128)(2,1)S(1)} %bitcast.8, f32[2,128]{1,0:T(2,128)S(1)} %bitcast.9, ...), custom_call_target="tpu_custom_call" | custom-call | tf_op jit(solution)/shard_map/chain/pallas_call | solution.py:316
  142.8 5.8 %weight_grads.1 = (f32[4096,512]{1,0:T(8,128)}, bf16[256,512]{1,0:T(8,128)(2,1)}, f32[1,512]{1,0:T(1,128)}, f32[2,128]{1,0:T(2,128)}) custom-call(bf16[256,4096]{1,0:T(8,128)(2,1)S(1)} %get-tuple-element.13.normed, bf16[256,512]{1,0:T(8,128)(2,1)S(1)} %get-tuple-element.14.carry, bf16[256,512]{1,0:T(8,128)(2,1)S(1)} %get-tuple-element.15.grads, ...), custom_call_target="tpu_custom_call" | custom-call | tf_op jit(solution)/shard_map/weight_grads/pallas_call | solution.py:368
Async XLA Ops:
  0.6 1.0 copy-start
  1.6 0.9 copy-start.1
  2.5 0.7 copy-start.2
  3.3 0.7 copy-start.3

commit v2 on v1

--- a/solution.py
+++ b/solution.py
@@ -12,8 +12,14 @@
 BF16 = jnp.bfloat16
 CHUNK = 16
 GROUP = 64
-FAR_FIRST = (5, 4, 3, 7, 2, 6, 1)
+FAR_FIRST = (5, 4, 3, 7, 2, 6, 1, 0)
+BATCHES = (0, 1, 4, 8)
+BACK = 4
 LAG = 3
+GATHERED = (1,)
+PROJECTED = (1, 2, 3)
+WRITES = 4
+VMEM_LIMIT = 48 << 20
 
 
 def wide(block, times):
@@ -22,22 +28,39 @@
 
 def chain_kernel(
     sections, n_dp, rows, cols,
-    cot_ref, x_ref, r_ref, gain_ref, w_hbm,
-    carry, gout, ggrad, rdot, normed_hbm,
+    cot_hbm, x_hbm, r_hbm, gain_hbm, w_hbm,
+    carry_hbm, gout_hbm, ggrad, rdot, turned_hbm,
+    x_ref, r_ref, gain_ref, carry, gout, turned,
     w, wt, xg, normed, u, xprev, rb, sb, rq, qbuf, g1, g1r, stat, statr,
-    w_sem, xg_send, xg_recv, xp_send, xp_recv, rq_recv, q_send, back_send, back_recv,
-    g1_send, g1_recv, st_send, st_recv, n_sem,
+    in_sem, w_sem, xg_send, xg_recv, xp_send, xp_recv, rq_recv, q_send, back_send, back_recv,
+    g1_send, g1_recv, st_send, st_recv, out_sem,
 ):
     s, d = lax.axis_index("section"), lax.axis_index("dp")
-    last = sections - 1
     chunks, groups = rows // CHUNK, rows // GROUP
     width = n_dp * cols
+    lanes = rb.shape[1]
+    last = sections - 1
     nxt = jnp.minimum(s + 1, last)
     prev = jnp.maximum(s - 1, 0)
-    lanes = rb.shape[1]
 
     def peer(i):
         return (d + i) % n_dp
+
+    def partner(off):
+        return d + off - 2 * sum(((d // b) % 2) * b for b in (1, 2, 4) if off & b)
+
+    fetch = [
+        pltpu.make_async_copy(x_hbm, x_ref, in_sem.at[0]),
+        pltpu.make_async_copy(r_hbm, r_ref, in_sem.at[1]),
+        pltpu.make_async_copy(gain_hbm, gain_ref, in_sem.at[2]),
+    ]
+    for copy in fetch:
+        copy.start()
+    first_carry = pltpu.make_async_copy(cot_hbm, carry, in_sem.at[3])
+
+    @pl.when(s == 0)
+    def _():
+        first_carry.start()
 
     def w_copy(k):
         part = pl.ds(pl.multiple_of(k * cols, cols), cols)
@@ -65,6 +88,9 @@
         def _(i):
             pl.semaphore_signal(barrier, inc=1, device_id=(nxt, i), device_id_type=MESH)
 
+    for copy in fetch:
+        copy.wait()
+
     for m in range(rows // lanes):
         rb[pl.ds(m * lanes, lanes), :] = jnp.broadcast_to(r_ref[pl.ds(m, 1), :], (lanes, lanes)).T
     g1[...] = jnp.zeros_like(g1)
@@ -76,11 +102,16 @@
     inner = jnp.logical_and(s > 0, s < last)
     pl.semaphore_wait(barrier, jnp.where(inner, 3 * n_dp - 1, 2 * n_dp - 1))
 
+    @pl.when(s < last)
+    def _():
+        pltpu.make_async_remote_copy(
+            x_ref, xprev, xp_send, xp_recv, device_id=(nxt, d), device_id_type=MESH
+        ).start()
+
     def group_rows(g):
         return pl.ds(pl.multiple_of(g * GROUP, GROUP), GROUP)
 
-    @pl.loop(0, groups)
-    def _(g):
+    def gather(g):
         part = group_rows(g)
         pltpu.make_async_copy(x_ref.at[part, :], xg.at[d, part, :], xg_recv.at[g]).start()
 
@@ -91,11 +122,17 @@
                 device_id=(s, peer(i)), device_id_type=MESH,
             ).start()
 
-    @pl.when(s < last)
-    def _():
-        pltpu.make_async_remote_copy(
-            x_ref, xprev, xp_send, xp_recv, device_id=(nxt, d), device_id_type=MESH
-        ).start()
+    def by_section(table):
+        amount = jnp.int32(groups)
+        for chip, some in reversed(list(enumerate(table))):
+            amount = jnp.where(s // 2 == chip, some, amount)
+        return amount
+
+    ahead, early = by_section(GATHERED), by_section(PROJECTED)
+
+    @pl.loop(0, ahead)
+    def _(g):
+        gather(g)
 
     @pl.loop(0, n_dp)
     def _(k):
@@ -115,14 +152,25 @@
                 xg[k, part, :].astype(F32) * scale * gain_ref[:, block]
             ).astype(BF16)
 
-        pltpu.make_async_copy(normed.at[part, :], normed_hbm.at[part, :], n_sem.at[g]).start()
         u[part, :] = jnp.dot(normed[part, :], w[...], preferred_element_type=F32)
-
-    early = jnp.where(s < 6, 1, groups)
 
     @pl.loop(0, early)
     def _(g):
         project(g)
+
+    turned_out = pltpu.make_async_copy(turned, turned_hbm, out_sem.at[0])
+
+    def turn():
+        @pl.loop(0, n_dp)
+        def _(k):
+            block = pl.ds(pl.multiple_of(k * cols, cols), cols)
+            turned[block, :] = normed[:, block].T
+
+        turned_out.start()
+
+    @pl.when(early == groups)
+    def _():
+        turn()
 
     def chunk_rows(i):
         return pl.ds(pl.multiple_of(i * CHUNK, CHUNK), CHUNK)
@@ -145,91 +193,98 @@
         gout[part, :] = result
         add_gain(g1r, x_ref[part, :], added)
 
-    @pl.when(s > 0)
-    def _():
-        pltpu.make_async_copy(xprev, xprev, xp_recv).wait()
-
-    @pl.loop(0, chunks)
-    def _(i):
+    def send(i):
         part = chunk_rows(i)
-
-        @pl.when(s == 0)
-        def _():
-            carry[part, :] = cot_ref[part, :]
-
-        @pl.when(s > 0)
-        def _():
-            added, result = total(i)
-            carry[part, :] = result
-            pltpu.make_async_remote_copy(
-                carry.at[part, :], gout.at[part, :], back_send, back_recv,
-                device_id=(prev, d), device_id_type=MESH,
-            ).start()
-            add_gain(g1, xprev[part, :], added)
-
         slot = jnp.where(s == last, chunks + i, i)
-
-        @pl.when(s < last)
-        def _():
-            pltpu.make_async_remote_copy(
-                carry.at[part, :], rq.at[slot, n_dp], q_send, rq_recv.at[slot],
-                device_id=(nxt, d), device_id_type=MESH,
-            ).start()
-
-        @pl.when(s == last)
-        def _():
-            pltpu.make_async_copy(carry.at[part, :], rq.at[slot, n_dp], rq_recv.at[slot]).start()
-
         mine = carry[part, :]
         scale = rb[part, :]
-        dots = mine.astype(F32) * u[part, :]
-        row = jnp.sum(dots, axis=1, keepdims=True) * (1.0 / width)
+        row = jnp.sum(mine.astype(F32) * u[part, :], axis=1, keepdims=True) * (1.0 / width)
         row = jnp.broadcast_to(row, (CHUNK, lanes))
         sb[part, :] = row
         shift = wide(row * scale * scale, cols // lanes)
         scale = wide(scale, cols // lanes)
-
-        def sums(f):
-            block = pl.ds(pl.multiple_of(f * cols, cols), cols)
-            product = jnp.dot(mine, wt[:, block], preferred_element_type=F32)
-            qbuf[i, f] = (
-                product * scale * gain_ref[:, block] - xg[f, part, :].astype(F32) * shift
-            ).astype(BF16)
-
-        for off in FAR_FIRST:
-            f = d + off - 2 * sum(((d // b) % 2) * b for b in (1, 2, 4) if off & b)
-            sums(f)
-            pltpu.make_async_remote_copy(
-                qbuf.at[i, f], rq.at[slot, d], q_send, rq_recv.at[slot],
-                device_id=(nxt, f), device_id_type=MESH,
-            ).start()
-        sums(d)
+        qbuf[i, n_dp] = mine
+        for first, end in zip(BATCHES, BATCHES[1:]):
+            for o in range(first, end):
+                f = partner(FAR_FIRST[o])
+                block = pl.ds(pl.multiple_of(f * cols, cols), cols)
+                product = jnp.dot(mine, wt[:, block], preferred_element_type=F32)
+                qbuf[i, o] = (
+                    product * scale * gain_ref[:, block] - xg[f, part, :].astype(F32) * shift
+                ).astype(BF16)
+            for o in range(first, min(end, n_dp - 1)):
+                pltpu.make_async_remote_copy(
+                    qbuf.at[i, o], rq.at[slot, o], q_send, rq_recv.at[slot],
+                    device_id=(nxt, partner(FAR_FIRST[o])), device_id_type=MESH,
+                ).start()
+        own = pl.ds(n_dp - 1, 2)
 
         @pl.when(s < last)
         def _():
             pltpu.make_async_remote_copy(
-                qbuf.at[i, d], rq.at[slot, d], q_send, rq_recv.at[slot],
+                qbuf.at[i, own], rq.at[slot, own], q_send, rq_recv.at[slot],
                 device_id=(nxt, d), device_id_type=MESH,
             ).start()
 
         @pl.when(s == last)
         def _():
-            pltpu.make_async_copy(qbuf.at[i, d], rq.at[slot, d], rq_recv.at[slot]).start()
-
+            pltpu.make_async_copy(qbuf.at[i, own], rq.at[slot, own], rq_recv.at[slot]).start()
+
+    def staged(i):
         per = GROUP // CHUNK
-
-        @pl.when(jnp.logical_and(early == 1, jnp.logical_and(i % per == per // 2, i // per + 1 < groups)))
+        g = i // per + 1
+
+        @pl.when(jnp.logical_and(i % per == 0, jnp.logical_and(g >= ahead, g < groups)))
         def _():
-            project(i // per + 1)
-
-        @pl.when(jnp.logical_and(s == last, i >= LAG))
+            gather(g)
+
+        @pl.when(jnp.logical_and(i % per == per - 1, jnp.logical_and(g >= early, g < groups)))
         def _():
-            finish(i - LAG)
+            project(g)
+
+    @pl.when(s == 0)
+    def _():
+        first_carry.wait()
+
+        @pl.loop(0, chunks)
+        def _(i):
+            send(i)
+            staged(i)
+
+    @pl.when(s > 0)
+    def _():
+        pltpu.make_async_copy(xprev, xprev, xp_recv).wait()
+
+        @pl.loop(0, chunks)
+        def _(i):
+            part = chunk_rows(i)
+            added, result = total(i)
+            carry[part, :] = result
+            send(i)
+            add_gain(g1, xprev[part, :], added)
+
+            @pl.when(i % BACK == BACK - 1)
+            def _():
+                several = pl.ds(
+                    pl.multiple_of((i - BACK + 1) * CHUNK, BACK * CHUNK), BACK * CHUNK
+                )
+                pltpu.make_async_remote_copy(
+                    carry.at[several, :], gout.at[several, :], back_send, back_recv,
+                    device_id=(prev, d), device_id_type=MESH,
+                ).start()
+
+            staged(i)
+
+            @pl.when(jnp.logical_and(s == last, i >= LAG))
+            def _():
+                finish(i - LAG)
+
+    carry_out = pltpu.make_async_copy(carry, carry_hbm, out_sem.at[1])
+    carry_out.start()
 
     stat[...] = jnp.zeros_like(stat)
     for m in range(rows // lanes):
-        turned = sb[pl.ds(m * lanes, lanes), :].T
-        stat[pl.ds(m, 1), :] = turned[0:1, :]
+        stat[pl.ds(m, 1), :] = sb[pl.ds(m * lanes, lanes), :].T[0:1, :]
 
     pltpu.make_async_copy(stat, statr.at[d], st_recv).start()
 
@@ -244,13 +299,10 @@
         pltpu.make_async_remote_copy(
             g1, g1r, g1_send, g1_recv, device_id=(prev, d), device_id_type=MESH
         ).start()
-        pltpu.make_async_copy(g1, g1, g1_send).wait()
-
-    @pl.when(s == last)
-    def _():
-        @pl.loop(chunks - LAG, chunks)
-        def _(i):
-            finish(i)
+
+    @pl.when(early < groups)
+    def _():
+        turn()
 
     pltpu.make_async_copy(statr, statr, st_recv).wait()
     rows_stat = statr[0]
@@ -271,9 +323,17 @@
 
     @pl.when(s < last)
     def _():
+        pltpu.make_async_copy(gout, gout, back_recv).wait()
         pltpu.make_async_copy(g1r, g1r, g1_recv).wait()
-        pltpu.make_async_copy(gout, gout, back_recv).wait()
-
+
+    @pl.when(s == last)
+    def _():
+        @pl.loop(chunks - LAG, chunks)
+        def _(i):
+            finish(i)
+
+    gout_out = pltpu.make_async_copy(gout, gout_hbm, out_sem.at[2])
+    gout_out.start()
     ggrad[...] = (
         jnp.sum(second + g1r[...], axis=0, keepdims=True)
         * (float(rows) ** -0.5)
@@ -289,7 +349,7 @@
     @pl.when(s < last)
     def _():
         sent(x_ref, xp_send)
-        sent(rq.at[pl.ds(0, chunks)], q_send)
+        sent(qbuf, q_send)
 
     @pl.when(s == last)
     def _():
@@ -298,11 +358,11 @@
     @pl.when(s > 0)
     def _():
         sent(carry, back_send)
-
-    @pl.loop(0, groups)
-    def _(g):
-        part = group_rows(g)
-        pltpu.make_async_copy(normed.at[part, :], normed_hbm.at[part, :], n_sem.at[g]).wait()
+        sent(g1, g1_send)
+
+    turned_out.wait()
+    carry_out.wait()
+    gout_out.wait()
 
 
 def chain(n_sec, n_dp, cotangent, x, scales, gain, weight):
@@ -321,11 +381,17 @@
             jax.ShapeDtypeStruct((rows, cols), BF16),
             jax.ShapeDtypeStruct((1, cols), F32),
             jax.ShapeDtypeStruct(scales.shape, F32),
-            jax.ShapeDtypeStruct((rows, width), BF16),
-        ),
-        in_specs=[vmem, vmem, vmem, vmem, hbm],
-        out_specs=(vmem, vmem, vmem, vmem, hbm),
+            jax.ShapeDtypeStruct((width, rows), BF16),
+        ),
+        in_specs=[pl.BlockSpec(memory_space=pltpu.HBM)] * 5,
+        out_specs=(hbm, hbm, vmem, vmem, hbm),
         scratch_shapes=[
+            pltpu.VMEM((rows, cols), BF16),
+            pltpu.VMEM(scales.shape, F32),
+            pltpu.VMEM((1, width), F32),
+            pltpu.VMEM((rows, cols), BF16),
+            pltpu.VMEM((rows, cols), BF16),
+            pltpu.VMEM((width, rows), BF16),
             pltpu.VMEM((width, cols), BF16),
             pltpu.VMEM((cols, width), BF16),
             pltpu.VMEM((n_dp, rows, cols), BF16),
@@ -335,24 +401,22 @@
             pltpu.VMEM((rows, lanes), F32),
             pltpu.VMEM((rows, lanes), F32),
             pltpu.VMEM((2 * chunks, n_dp + 1, CHUNK, cols), BF16),
-            pltpu.VMEM((chunks, n_dp, CHUNK, cols), BF16),
+            pltpu.VMEM((chunks, n_dp + 1, CHUNK, cols), BF16),
             pltpu.VMEM((8, cols), F32),
             pltpu.VMEM((8, cols), F32),
             pltpu.VMEM((8, lanes), F32),
             pltpu.VMEM((n_dp, 8, lanes), F32),
-            sem((n_dp,)), sem, sem((groups,)), sem, sem, sem((2 * chunks,)), sem, sem, sem,
-            sem, sem, sem, sem, sem((groups,)),
+            sem((4,)), sem((n_dp,)), sem, sem((groups,)), sem, sem, sem((2 * chunks,)), sem, sem, sem,
+            sem, sem, sem, sem, sem((3,)),
         ],
         compiler_params=pltpu.CompilerParams(
-            collective_id=0, has_side_effects=True, vmem_limit_bytes=48 << 20
+            collective_id=0, has_side_effects=True, vmem_limit_bytes=VMEM_LIMIT
         ),
     )(cotangent, x, scales, gain, weight)
 
 
 def weight_kernel(scale, normed, carry, grads, gain_grad, row_dot, w_out, g_out, gg_out, rd_out):
-    w_out[...] = scale * lax.dot_general(
-        normed[...], carry[...], (((0,), (0,)), ((), ())), preferred_element_type=F32
-    )
+    w_out[...] = scale * jnp.dot(normed[...], carry[...], preferred_element_type=F32)
 
     @pl.when(pl.program_id(0) == 0)
     def _():
@@ -362,13 +426,14 @@
 
 
 def weight_grads(normed, carry, grads, gain_grad, row_dot):
-    rows, width = normed.shape
+    width, rows = normed.shape
     cols = carry.shape[1]
+    part = width // WRITES
     whole = lambda a: pl.BlockSpec(a.shape, lambda k: (0, 0))
     return pl.pallas_call(
         functools.partial(weight_kernel, float(rows) ** -0.5),
         name="weight_grads",
-        grid=(width // cols,),
+        grid=(WRITES,),
         out_shape=(
             jax.ShapeDtypeStruct((width, cols), F32),
             jax.ShapeDtypeStruct(grads.shape, grads.dtype),
@@ -376,14 +441,14 @@
             jax.ShapeDtypeStruct(row_dot.shape, F32),
         ),
         in_specs=[
-            pl.BlockSpec((rows, cols), lambda k: (0, k)),
+            pl.BlockSpec((part, rows), lambda k: (k, 0)),
             whole(carry), whole(grads), whole(gain_grad), whole(row_dot),
         ],
         out_specs=(
-            pl.BlockSpec((cols, cols), lambda k: (k, 0)),
+            pl.BlockSpec((part, cols), lambda k: (k, 0)),
             whole(grads), whole(gain_grad), whole(row_dot),
         ),
-        compiler_params=pltpu.CompilerParams(vmem_limit_bytes=24 << 20),
+        compiler_params=pltpu.CompilerParams(vmem_limit_bytes=VMEM_LIMIT),
     )(normed, carry, grads, gain_grad, row_dot)
 
 

time: 149 us -> 136 us (0.913)
  Pallas kernels: 145 us -> 132 us
    pallas_call x1, Pallas kernels: 139 us -> 128 us  [chain(): pl.pallas_call(functools.partial(chain_kernel, n_sec, n_dp, rows, cols),...]
    pallas_call x1, Pallas kernels: 5.76 us -> 4.26 us  [weight_grads(): pl.pallas_call(functools.partial(weight_kernel, float(rows) ** (-0.5)), n...]
where the time goes in v2:
time: 136 us
  Pallas kernels  132 us (97%)
  local copies, waits for them, and re-layouts  3.29 us (2%)
    pallas_call x1, Pallas kernels, chain(): pl.pallas_call(functools.partial(chain_kernel, n_sec, n_dp, rows, cols),...  128 us
    pallas_call x1, Pallas kernels, weight_grads(): pl.pallas_call(functools.partial(weight_kernel, float(rows) ** (-0.5)), n...  4.26 us
    unnamed x8, local copies, waits for them, and re-layouts  3.29 us

profile of v2, /device:TPU:23, one launch (start us, length us, event | category | flops | bytes accessed | tf_op | source)
XLA Modules:
  0.0 136.2 jit_solution(13451095338046181673)
XLA Ops:
  0.6 0.0 copy-start
  0.6 0.9 copy-done
  1.6 0.0 copy-start.1
  1.6 0.9 copy-done.1
  2.5 0.0 copy-start.2
  2.5 0.7 copy-done.2
  3.3 0.0 copy-start.3
  3.3 0.7 copy-done.3
  3.9 128.0 %chain.1 = (bf16[256,512]{1,0:T(8,128)(2,1)S(1)}, bf16[256,512]{1,0:T(8,128)(2,1)S(1)}, f32[1,512]{1,0:T(1,128)S(1)}, f32[2,128]{1,0:T(2,128)S(1)}, bf16[4096,256]{1,0:T(8,128)(2,1)S(1)}) custom-call(bf16[256,512]{1,0:T(8,128)(2,1)S(1)} %bitcast.7, bf16[256,512]{1,0:T(8,128)(2,1)S(1)} %bitcast.8, f32[2,128]{1,0:T(2,128)S(1)} %bitcast.9, ...), custom_call_target="tpu_custom_call" | custom-call | tf_op jit(solution)/shard_map/chain/pallas_call | solution.py:376
  131.9 4.3 %weight_grads.1 = (f32[4096,512]{1,0:T(8,128)}, bf16[256,512]{1,0:T(8,128)(2,1)}, f32[1,512]{1,0:T(1,128)}, f32[2,128]{1,0:T(2,128)}) custom-call(bf16[4096,256]{1,0:T(8,128)(2,1)S(1)} %get-tuple-element.13.normed, bf16[256,512]{1,0:T(8,128)(2,1)S(1)} %get-tuple-element.14.carry, bf16[256,512]{1,0:T(8,128)(2,1)S(1)} %get-tuple-element.15.grads, ...), custom_call_target="tpu_custom_call" | custom-call | tf_op jit(solution)/shard_map/weight_grads/pallas_call | solution.py:433
Async XLA Ops:
  0.6 1.0 copy-start
  1.6 0.9 copy-start.1
  2.5 0.7 copy-start.2
  3.3 0.7 copy-start.3

commit v3 on v2

--- a/solution.py
+++ b/solution.py
@@ -15,9 +15,8 @@
 FAR_FIRST = (5, 4, 3, 7, 2, 6, 1, 0)
 BATCHES = (0, 1, 4, 8)
 BACK = 4
-LAG = 3
-GATHERED = (1,)
-PROJECTED = (1, 2, 3)
+LAG = 5
+PROJECTED = (1, 3)
 WRITES = 4
 VMEM_LIMIT = 48 << 20
 
@@ -28,7 +27,7 @@
 
 def chain_kernel(
     sections, n_dp, rows, cols,
-    cot_hbm, x_hbm, r_hbm, gain_hbm, w_hbm,
+    blocks_hbm, scales_hbm, w_hbm,
     carry_hbm, gout_hbm, ggrad, rdot, turned_hbm,
     x_ref, r_ref, gain_ref, carry, gout, turned,
     w, wt, xg, normed, u, xprev, rb, sb, rq, qbuf, g1, g1r, stat, statr,
@@ -50,13 +49,13 @@
         return d + off - 2 * sum(((d // b) % 2) * b for b in (1, 2, 4) if off & b)
 
     fetch = [
-        pltpu.make_async_copy(x_hbm, x_ref, in_sem.at[0]),
-        pltpu.make_async_copy(r_hbm, r_ref, in_sem.at[1]),
-        pltpu.make_async_copy(gain_hbm, gain_ref, in_sem.at[2]),
+        pltpu.make_async_copy(blocks_hbm.at[pl.ds(rows, rows), :], x_ref, in_sem.at[0]),
+        pltpu.make_async_copy(scales_hbm.at[:, pl.ds(width, rows)], r_ref, in_sem.at[1]),
+        pltpu.make_async_copy(scales_hbm.at[:, pl.ds(0, width)], gain_ref, in_sem.at[2]),
     ]
     for copy in fetch:
         copy.start()
-    first_carry = pltpu.make_async_copy(cot_hbm, carry, in_sem.at[3])
+    first_carry = pltpu.make_async_copy(blocks_hbm.at[pl.ds(0, rows), :], carry, in_sem.at[3])
 
     @pl.when(s == 0)
     def _():
@@ -92,7 +91,7 @@
         copy.wait()
 
     for m in range(rows // lanes):
-        rb[pl.ds(m * lanes, lanes), :] = jnp.broadcast_to(r_ref[pl.ds(m, 1), :], (lanes, lanes)).T
+        rb[pl.ds(m * lanes, lanes), :] = jnp.broadcast_to(r_ref[:, pl.ds(m * lanes, lanes)], (lanes, lanes)).T
     g1[...] = jnp.zeros_like(g1)
 
     @pl.when(s == last)
@@ -111,16 +110,61 @@
     def group_rows(g):
         return pl.ds(pl.multiple_of(g * GROUP, GROUP), GROUP)
 
-    def gather(g):
+    up, down, side = (d + 2) % n_dp, (d + n_dp - 2) % n_dp, partner(1)
+    across = (d + n_dp // 2) % n_dp
+
+    def pass_on(source, owner, part, target, semaphore):
+        pltpu.make_async_remote_copy(
+            source, xg.at[owner, part, :], xg_send, semaphore,
+            device_id=(s, target), device_id_type=MESH,
+        ).start()
+
+    def arrived(blocks, g, semaphore):
+        amount = xg.at[pl.ds(0, blocks), group_rows(g), :]
+        pltpu.make_async_copy(amount, amount, semaphore).wait()
+
+    def first_pass(g):
         part = group_rows(g)
-        pltpu.make_async_copy(x_ref.at[part, :], xg.at[d, part, :], xg_recv.at[g]).start()
-
-        @pl.loop(1, n_dp)
-        def _(i):
-            pltpu.make_async_remote_copy(
-                x_ref.at[part, :], xg.at[d, part, :], xg_send, xg_recv.at[g],
-                device_id=(s, peer(i)), device_id_type=MESH,
-            ).start()
+
+        @pl.when(g == 0)
+        def _():
+            pass_on(x_ref.at[part, :], d, part, side, xg_recv.at[2, g])
+            for target in (partner(5), across):
+                pass_on(x_ref.at[part, :], d, part, target, xg_recv.at[0, g])
+
+        @pl.when(g > 0)
+        def _():
+            pass_on(x_ref.at[part, :], d, part, side, xg_recv.at[0, g])
+
+        pltpu.make_async_copy(x_ref.at[part, :], xg.at[d, part, :], xg_recv.at[0, g]).start()
+        for target in (up, down):
+            pass_on(x_ref.at[part, :], d, part, target, xg_recv.at[0, g])
+
+    def second_pass(g):
+        part = group_rows(g)
+
+        @pl.when(g == 0)
+        def _():
+            arrived(1, g, xg_recv.at[2, g])
+
+        @pl.when(g > 0)
+        def _():
+            arrived(4, g, xg_recv.at[0, g])
+            half = GROUP // 2
+            low = pl.ds(pl.multiple_of(g * GROUP, half), half)
+            high = pl.ds(pl.multiple_of(g * GROUP + half, half), half)
+            pass_on(xg.at[down, low, :], down, low, up, xg_recv.at[1, g])
+            pass_on(xg.at[up, high, :], up, high, down, xg_recv.at[1, g])
+
+        for target in (up, down):
+            pass_on(xg.at[side, part, :], side, part, target, xg_recv.at[1, g])
+
+    def third_pass(g):
+        @pl.when(g > 0)
+        def _():
+            arrived(3, g, xg_recv.at[1, g])
+            part = group_rows(g)
+            pass_on(xg.at[across, part, :], across, part, side, xg_recv.at[2, g])
 
     def by_section(table):
         amount = jnp.int32(groups)
@@ -128,11 +172,10 @@
             amount = jnp.where(s // 2 == chip, some, amount)
         return amount
 
-    ahead, early = by_section(GATHERED), by_section(PROJECTED)
-
-    @pl.loop(0, ahead)
-    def _(g):
-        gather(g)
+    early = by_section(PROJECTED)
+    passes = ((first_pass, 2), (second_pass, 1), (third_pass, 0))
+
+    first_pass(0)
 
     @pl.loop(0, n_dp)
     def _(k):
@@ -140,9 +183,25 @@
         part = pl.ds(pl.multiple_of(k * cols, cols), cols)
         wt[:, part] = w[part, :].T
 
+    @pl.loop(1, early + 2)
+    def _(k):
+        for late, (one, more) in enumerate(passes):
+            @pl.when(jnp.logical_and(k >= late, k - late < jnp.minimum(early + more, groups)))
+            def _():
+                one(k - late)
+
     def project(g):
         part = group_rows(g)
-        pltpu.make_async_copy(xg.at[:, part, :], xg.at[:, part, :], xg_recv.at[g]).wait()
+
+        @pl.when(g == 0)
+        def _():
+            arrived(5, g, xg_recv.at[0, g])
+            arrived(2, g, xg_recv.at[1, g])
+
+        @pl.when(g > 0)
+        def _():
+            arrived(1, g, xg_recv.at[2, g])
+
         scale = wide(rb[part, :], cols // lanes)
 
         @pl.loop(0, n_dp)
@@ -232,15 +291,14 @@
 
     def staged(i):
         per = GROUP // CHUNK
-        g = i // per + 1
-
-        @pl.when(jnp.logical_and(i % per == 0, jnp.logical_and(g >= ahead, g < groups)))
-        def _():
-            gather(g)
-
-        @pl.when(jnp.logical_and(i % per == per - 1, jnp.logical_and(g >= early, g < groups)))
-        def _():
-            project(g)
+        for at, one, more in (
+            (0, third_pass, 0), (1, first_pass, 2), (2, second_pass, 1), (3, project, 0)
+        ):
+            g = i // per + 1 + more
+
+            @pl.when(jnp.logical_and(i % per == at, jnp.logical_and(g >= early + more, g < groups)))
+            def _():
+                one(g)
 
     @pl.when(s == 0)
     def _():
@@ -309,7 +367,10 @@
     for k in range(1, n_dp):
         rows_stat += statr[k]
     halves = rows // lanes
-    rdot[...] = rows_stat[:halves, :] * (float(width) ** 0.5) / r_ref[...]
+    for m in range(halves):
+        rdot[pl.ds(m, 1), :] = (
+            rows_stat[m : m + 1, :] * (float(width) ** 0.5) / r_ref[:, pl.ds(m * lanes, lanes)]
+        )
 
     own = pl.ds(pl.multiple_of(d * cols, cols), cols)
     second = jnp.zeros((8, cols), F32)
@@ -369,6 +430,8 @@
     rows, cols = x.shape
     width = n_dp * cols
     lanes = scales.shape[1]
+    blocks = jnp.concatenate([cotangent, x], axis=0)
+    factors = jnp.concatenate([gain, scales.reshape(1, rows)], axis=1)
     chunks, groups = rows // CHUNK, rows // GROUP
     vmem = pl.BlockSpec(memory_space=pltpu.VMEM)
     hbm = pl.BlockSpec(memory_space=pl.ANY)
@@ -383,11 +446,11 @@
             jax.ShapeDtypeStruct(scales.shape, F32),
             jax.ShapeDtypeStruct((width, rows), BF16),
         ),
-        in_specs=[pl.BlockSpec(memory_space=pltpu.HBM)] * 5,
+        in_specs=[hbm] * 3,
         out_specs=(hbm, hbm, vmem, vmem, hbm),
         scratch_shapes=[
             pltpu.VMEM((rows, cols), BF16),
-            pltpu.VMEM(scales.shape, F32),
+            pltpu.VMEM((1, rows), F32),
             pltpu.VMEM((1, width), F32),
             pltpu.VMEM((rows, cols), BF16),
             pltpu.VMEM((rows, cols), BF16),
@@ -406,13 +469,13 @@
             pltpu.VMEM((8, cols), F32),
             pltpu.VMEM((8, lanes), F32),
             pltpu.VMEM((n_dp, 8, lanes), F32),
-            sem((4,)), sem((n_dp,)), sem, sem((groups,)), sem, sem, sem((2 * chunks,)), sem, sem, sem,
+            sem((4,)), sem((n_dp,)), sem, sem((3, groups)), sem, sem, sem((2 * chunks,)), sem, sem, sem,
             sem, sem, sem, sem, sem((3,)),
         ],
         compiler_params=pltpu.CompilerParams(
             collective_id=0, has_side_effects=True, vmem_limit_bytes=VMEM_LIMIT
         ),
-    )(cotangent, x, scales, gain, weight)
+    )(blocks, factors, weight)
 
 
 def weight_kernel(scale, normed, carry, grads, gain_grad, row_dot, w_out, g_out, gg_out, rd_out):

time: 136 us -> 131 us (0.963)
  Pallas kernels: 132 us -> 128 us
  local copies, waits for them, and re-layouts: 3.29 us -> 0 us
  other arithmetic: 0 us -> 1.82 us
    pallas_call x1, Pallas kernels: 128 us -> 124 us  [chain(): pl.pallas_call(functools.partial(chain_kernel, n_sec, n_dp, rows, cols),...]
    unnamed x8 -> x0, local copies, waits for them, and re-layouts: 3.29 us -> none
    concatenate x0 -> x2, other arithmetic: none -> 1.82 us  [the longest x1 1.07 us: chain(): blocks = jnp.concatenate([cotangent, x], axis=0)]
where the time goes in v3:
time: 131 us; the launch traced here: 130 us
  Pallas kernels  128 us (98%)
  other arithmetic  1.82 us (1%)
    pallas_call x1, Pallas kernels, chain(): pl.pallas_call(functools.partial(chain_kernel, n_sec, n_dp, rows, cols),...  124 us
    pallas_call x1, Pallas kernels, weight_grads(): pl.pallas_call(functools.partial(weight_kernel, float(rows) ** (-0.5)), n...  4.26 us

profile of v3, /device:TPU:23, one launch (start us, length us, event | category | flops | bytes accessed | tf_op | source)
XLA Modules:
  0.0 130.5 jit_solution(1015087596727486003)
XLA Ops:
  0.6 0.8 pad_maximum_fusion.1.scales_hbm
  1.4 1.1 pad_maximum_fusion.blocks_hbm
  2.5 123.8 %chain.1 = (bf16[256,512]{1,0:T(8,128)(2,1)S(1)}, bf16[256,512]{1,0:T(8,128)(2,1)S(1)}, f32[1,512]{1,0:T(1,128)S(1)}, f32[2,128]{1,0:T(2,128)S(1)}, bf16[4096,256]{1,0:T(8,128)(2,1)S(1)}) custom-call(bf16[512,512]{1,0:T(8,128)(2,1)S(1)} %pad_maximum_fusion.blocks_hbm, f32[1,4352]{1,0:T(1,128)S(1)} %pad_maximum_fusion.1.scales_hbm, bf16[4096,512]{1,0:T(8,128)(2,1)} %bitcast.7), custom_call_target="tpu_custom_call" | custom-call | tf_op jit(solution)/shard_map/chain/pallas_call | solution.py:439
  126.2 4.3 %weight_grads.1 = (f32[4096,512]{1,0:T(8,128)}, bf16[256,512]{1,0:T(8,128)(2,1)}, f32[1,512]{1,0:T(1,128)}, f32[2,128]{1,0:T(2,128)}) custom-call(bf16[4096,256]{1,0:T(8,128)(2,1)S(1)} %get-tuple-element.13.normed, bf16[256,512]{1,0:T(8,128)(2,1)S(1)} %get-tuple-element.14.carry, bf16[256,512]{1,0:T(8,128)(2,1)S(1)} %get-tuple-element.15.grads, ...), custom_call_target="tpu_custom_call" | custom-call | tf_op jit(solution)/shard_map/weight_grads/pallas_call | solution.py:496

commit v4 on v3

--- a/solution.py
+++ b/solution.py
@@ -12,12 +12,12 @@
 BF16 = jnp.bfloat16
 CHUNK = 16
 GROUP = 64
-FAR_FIRST = (5, 4, 3, 7, 2, 6, 1, 0)
-BATCHES = (0, 1, 4, 8)
+FAR_FIRST = (5, 4, 7, 3, 6, 2, 1, 0)
+BATCHES = (0, 2, 4, 6, 8)
 BACK = 4
 LAG = 5
 PROJECTED = (1, 3)
-WRITES = 4
+WRITES = 2
 VMEM_LIMIT = 48 << 20
 
 

time: 131 us -> 129 us (0.985)
  Pallas kernels: 128 us -> 126 us
    pallas_call x1, Pallas kernels: 124 us -> 122 us  [chain(): pl.pallas_call(functools.partial(chain_kernel, n_sec, n_dp, rows, cols),...]
where the time goes in v4:
time: 129 us
  Pallas kernels  126 us (98%)
  other arithmetic  1.82 us (1%)
    pallas_call x1, Pallas kernels, chain(): pl.pallas_call(functools.partial(chain_kernel, n_sec, n_dp, rows, cols),...  122 us
    pallas_call x1, Pallas kernels, weight_grads(): pl.pallas_call(functools.partial(weight_kernel, float(rows) ** (-0.5)), n...  4.15 us

profile of v4, /device:TPU:23, one launch (start us, length us, event | category | flops | bytes accessed | tf_op | source)
XLA Modules:
  0.0 128.6 jit_solution(16318351410300250792)
XLA Ops:
  0.6 0.8 pad_maximum_fusion.1.scales_hbm
  1.4 1.1 pad_maximum_fusion.blocks_hbm
  2.5 121.9 %chain.1 = (bf16[256,512]{1,0:T(8,128)(2,1)S(1)}, bf16[256,512]{1,0:T(8,128)(2,1)S(1)}, f32[1,512]{1,0:T(1,128)S(1)}, f32[2,128]{1,0:T(2,128)S(1)}, bf16[4096,256]{1,0:T(8,128)(2,1)S(1)}) custom-call(bf16[512,512]{1,0:T(8,128)(2,1)S(1)} %pad_maximum_fusion.blocks_hbm, f32[1,4352]{1,0:T(1,128)S(1)} %pad_maximum_fusion.1.scales_hbm, bf16[4096,512]{1,0:T(8,128)(2,1)} %bitcast.7), custom_call_target="tpu_custom_call" | custom-call | tf_op jit(solution)/shard_map/chain/pallas_call | solution.py:439
  124.4 4.2 %weight_grads.1 = (f32[4096,512]{1,0:T(8,128)}, bf16[256,512]{1,0:T(8,128)(2,1)}, f32[1,512]{1,0:T(1,128)}, f32[2,128]{1,0:T(2,128)}) custom-call(bf16[4096,256]{1,0:T(8,128)(2,1)S(1)} %get-tuple-element.13.normed, bf16[256,512]{1,0:T(8,128)(2,1)S(1)} %get-tuple-element.14.carry, bf16[256,512]{1,0:T(8,128)(2,1)S(1)} %get-tuple-element.15.grads, ...), custom_call_target="tpu_custom_call" | custom-call | tf_op jit(solution)/shard_map/weight_grads/pallas_call | solution.py:496

commit v5 on v4

--- a/solution.py
+++ b/solution.py
@@ -13,10 +13,10 @@
 CHUNK = 16
 GROUP = 64
 FAR_FIRST = (5, 4, 7, 3, 6, 2, 1, 0)
-BATCHES = (0, 2, 4, 6, 8)
+BATCHES = (0, 2, 5, 8)
 BACK = 4
 LAG = 5
-PROJECTED = (1, 3)
+PROJECTED = (1, 2, 3)
 WRITES = 2
 VMEM_LIMIT = 48 << 20
 

time: 129 us -> 128 us (level)
  no operation moved by 1% of the time
where the time goes in v5:
time: 128 us
  Pallas kernels  125 us (98%)
  other arithmetic  1.82 us (1%)
    pallas_call x1, Pallas kernels, chain(): pl.pallas_call(functools.partial(chain_kernel, n_sec, n_dp, rows, cols),...  121 us
    pallas_call x1, Pallas kernels, weight_grads(): pl.pallas_call(functools.partial(weight_kernel, float(rows) ** (-0.5)), n...  4.14 us

profile of v5, /device:TPU:23, one launch (start us, length us, event | category | flops | bytes accessed | tf_op | source)
XLA Modules:
  0.0 127.6 jit_solution(5104189926319452600)
XLA Ops:
  0.6 0.8 pad_maximum_fusion.1.scales_hbm
  1.4 1.1 pad_maximum_fusion.blocks_hbm
  2.5 121.0 %chain.1 = (bf16[256,512]{1,0:T(8,128)(2,1)S(1)}, bf16[256,512]{1,0:T(8,128)(2,1)S(1)}, f32[1,512]{1,0:T(1,128)S(1)}, f32[2,128]{1,0:T(2,128)S(1)}, bf16[4096,256]{1,0:T(8,128)(2,1)S(1)}) custom-call(bf16[512,512]{1,0:T(8,128)(2,1)S(1)} %pad_maximum_fusion.blocks_hbm, f32[1,4352]{1,0:T(1,128)S(1)} %pad_maximum_fusion.1.scales_hbm, bf16[4096,512]{1,0:T(8,128)(2,1)} %bitcast.7), custom_call_target="tpu_custom_call" | custom-call | tf_op jit(solution)/shard_map/chain/pallas_call | solution.py:439
  123.4 4.1 %weight_grads.1 = (f32[4096,512]{1,0:T(8,128)}, bf16[256,512]{1,0:T(8,128)(2,1)}, f32[1,512]{1,0:T(1,128)}, f32[2,128]{1,0:T(2,128)}) custom-call(bf16[4096,256]{1,0:T(8,128)(2,1)S(1)} %get-tuple-element.13.normed, bf16[256,512]{1,0:T(8,128)(2,1)S(1)} %get-tuple-element.14.carry, bf16[256,512]{1,0:T(8,128)(2,1)S(1)} %get-tuple-element.15.grads, ...), custom_call_target="tpu_custom_call" | custom-call | tf_op jit(solution)/shard_map/weight_grads/pallas_call | solution.py:496
